TPU v7x, 32 devices: a whole 2x2x4 slice. The times are simulated.
32 devices in a mesh: seq: 16 (over z, y, x), tp: 2 (over core).
Axes of the slice: x: 2, y: 2, z: 4, core: 2. Of those that a mesh axis runs over, the one named last changes fastest.
Arguments:
- student: bfloat16 [4096, 2048], P('seq'), may hold values from -6 to 6
- projector: bfloat16 [2, 4224, 2048], P('tp', 'seq'), may hold values from -0.125 to 0.125
- teacher: bfloat16 [2, 4096, 8448], P(None, 'seq', 'tp'), may hold values from -6 to 6
- layer_index: int32 [4096], P('seq'), may hold values from 0 to 1
- valid_mask: int32 [4096], P('seq'), may hold values 0 or 1
Outputs:
- grad_student: bfloat16 [4096, 2048], P('seq', 'tp')
- token_loss: float32 [4096], P(('seq', 'tp'))
All inputs are finite; a program needn't handle non-finite values. No bound on the sum of `valid_mask` on one device may be relied on, other than what follows from the above.
Results may differ from a plain program's by a relative error of at most 0.0034.
Values may be sent and summed in bfloat16 or wider, within the bound.
A program may use at most 64 MiB of HBM per device.

v0:
```python
import jax
import jax.numpy as jnp
from jax import lax
from jax.sharding import PartitionSpec as P

HW = 8448


def body(student, projector, teacher, layer_index, valid_mask):
    rows_dev = student.shape[0]
    feat_dim = student.shape[1]
    chosen = teacher[0]
    chosen = jnp.where((layer_index == 1)[:, None], teacher[1], chosen)
    weight = valid_mask.astype(jnp.float32)[:, None]
    gathered = lax.all_gather(projector, "seq", axis=1, tiled=True)
    flat_rows = gathered.reshape(-1, feat_dim)
    predicted = lax.dot_general(
        student, flat_rows, (((1,), (1,)), ((), ())), preferred_element_type=jnp.float32
    )
    difference = predicted - chosen.astype(jnp.float32)
    masked_err = (weight * difference).astype(jnp.bfloat16)
    grad_term = jnp.dot(masked_err, flat_rows, preferred_element_type=jnp.float32)
    squares = jnp.sum(difference * difference, axis=1)
    summed, totals = (
        lax.psum_scatter(grad_term, "tp", scatter_dimension=1, tiled=True),
        lax.psum_scatter(squares, "tp", scatter_dimension=0, tiled=True),
    )
    tp_count = lax.axis_size("tp")
    share_rows = rows_dev // tp_count
    own_mask = lax.dynamic_slice_in_dim(
        valid_mask, lax.axis_index("tp") * share_rows, share_rows
    ).astype(jnp.float32)
    return (summed.astype(jnp.bfloat16), own_mask * totals / HW)


def solution(mesh):
    placed = (P("seq", None), P("tp", "seq", None), P(None, "seq", "tp"), P("seq"), P("seq"))
    return jax.shard_map(
        body,
        mesh=mesh,
        in_specs=placed,
        out_specs=(P("seq", "tp"), P(("seq", "tp"))),
        check_vma=False,
    )
```

profile of v0, /device:TPU:0, one launch (start us, length us, event | category | flops | bytes accessed | tf_op | source)
XLA Modules:
  0.0 260.1 jit_solution(11113816485252569042)
XLA Ops:
  7.2 0.0 copy-start
  7.2 0.0 all-gather.2.cloned.1.call-start
  7.2 0.7 all-gather.2.cloned.1.call-update
  7.9 0.0 reduce-scatter.2.cloned.1.call-start
  8.0 0.7 convert_element_type.15
  8.6 0.7 broadcast_compare_fusion
  9.3 200.8 %all-gather.2.cloned.1.call-done = bf16[1,4224,2048]{2,1,0:T(8,128)(2,1)} async-done(((bf16[1,264,2048]{2,1,0:T(8,128)(2,1)}), bf16[1,4224,2048]{2,1,0:T(8,128)(2,1)}) %all-gather.2.cloned.1.call-update) | async-done | bytes 17301520 | tf_op jit(solution)/shard_map/all_gather | solution.py:15
  210.2 0.0 copy-done
  210.2 19.6 %multiply_reduce_fusion = (f32[256]{0:T(256)S(1)}, f32[256,4224]{1,0:T(8,128)}) fusion(bf16[2,256,4224]{2,1,0:T(8,128)(2,1)} %param.7, pred[256]{0:T(512)(128)(4,1)S(1)} %broadcast_compare_fusion, bf16[256,2048]{1,0:T(8,128)(2,1)S(1)} %copy-done, bf16[1,4224,2048]{2,1,0:T(8,128)(2,1)} %all-gather.2.cloned.1.call-done), kind=kOutput, calls=%fused_computation.5 | convolution fusion | flops 4434591744 | bytes 27002112 | tf_op jit(solution)/shard_map/dot_general | solution.py:17
  229.8 0.0 copy-start.2
  229.8 0.0 copy-start.1
  229.8 13.4 %fusion = f32[256,2048]{1,0:T(8,128)} fusion(bf16[1,4224,2048]{2,1,0:T(8,128)(2,1)} %all-gather.2.cloned.1.call-done, f32[256,4224]{1,0:T(8,128)} %get-tuple-element.3, f32[256]{0:T(256)S(1)} %convert_element_type.15), kind=kOutput, calls=%fused_computation | convolution fusion | flops 4431347712 | bytes 23725056 | tf_op jit(solution)/shard_map/dot_general | solution.py:22
  243.2 0.0 reduce-scatter.2.cloned.1.call-update
  243.2 0.0 copy-done.2
  243.2 0.6 dynamic-slice
  244.5 2.5 all-reduce
  246.9 0.0 copy-done.1
  246.9 0.6 fusion.8
  247.5 3.6 %reduce-scatter.2.cloned.1.call-done = f32[256,1024]{1,0:T(8,128)} async-done(((f32[256,2048]{1,0:T(8,128)}), f32[256,1024]{1,0:T(8,128)}) %reduce-scatter.2.cloned.1.call-update) | async-done | bytes 1048592 | tf_op jit(solution)/shard_map/reduce_scatter | solution.py:25
  251.2 2.1 convert_element_type.18
Async XLA Ops:
  7.2 203.0 %copy-start = (bf16[256,2048]{1,0:T(8,128)(2,1)S(1)}, bf16[256,2048]{1,0:T(8,128)(2,1)}, u32[]{:S(2)}) copy-start(bf16[256,2048]{1,0:T(8,128)(2,1)} %param.5) | copy-start | bytes 3145732
  7.2 203.0 %all-gather.2.cloned.1.call-start = ((), (), s32[]{:S(2)}) async-start(), calls=%async_computation.1 | async-start | bytes 18382848 | tf_op jit(solution)/shard_map/all_gather | solution.py:15
  7.9 243.3 %reduce-scatter.2.cloned.1.call-start = ((), (), s32[]{:S(2)}) async-start(), calls=%async_computation.2 | async-start | bytes 3145728 | tf_op jit(solution)/shard_map/reduce_scatter | solution.py:25
  229.8 13.5 %copy-start.2 = (u32[32]{0:T(128)S(1)}, u32[32]{0:T(128)}, u32[]{:S(2)}) copy-start(u32[32]{0:T(128)} %constant.20) | copy-start | bytes 388
  229.8 17.2 %copy-start.1 = (s32[256]{0:T(256)S(1)}, s32[256]{0:T(256)}, u32[]{:S(2)}) copy-start(s32[256]{0:T(256)} %param.9) | copy-start | bytes 3076
Sparse Core Ops, SparseCore 0:
  10.8 199.3 all-gather.1
  243.3 7.7 reduce-scatter.1
where the time goes:
time: 260 us
  waiting for transfers between devices  205 us (79%)
  matrix products  33 us (13%)
  between operations  14.7 us (6%)
  other arithmetic  4.05 us (2%)
    all_gather x1, waiting for transfers between devices, body(): gathered = lax.all_gather(projector, 'seq', axis=1, tiled=True)  201 us
    dot_general x1, matrix products, body(): lax.dot_general(student, flat_rows, (((1,), (1,)), ((), ())), preferred_e...  19.6 us
    dot_general x1, matrix products, body(): jnp.dot(masked_err, flat_rows, preferred_element_type=jnp.float32)  13.4 us
  transfers between devices with their start and end apart: 2, of which 2 were waited for; matrix products, arithmetic and copies ran while one was open for 1% of the time, Pallas kernels for 0%

commit v1 on v0

--- a/solution.py
+++ b/solution.py
@@ -6,13 +6,34 @@
 HW = 8448
 
 
+def gather_around(shard, axis, dim):
+    size, index, width = (lax.axis_size(axis), lax.axis_index(axis), shard.shape[dim])
+    right = [(i, (i + 1) % size) for i in range(size)]
+    left = [(i, (i - 1) % size) for i in range(size)]
+    out = jnp.zeros((*shard.shape[:dim], size * width, *shard.shape[dim + 1 :]), shard.dtype)
+    out = lax.dynamic_update_slice_in_dim(out, shard, index * width, axis=dim)
+    from_left = from_right = shard
+    halfway = size // 2
+    for turn in range(1, halfway + 1):
+        from_left = lax.ppermute(from_left, axis, right)
+        out = lax.dynamic_update_slice_in_dim(
+            out, from_left, (index - turn) % size * width, axis=dim
+        )
+        if turn < size - halfway:
+            from_right = lax.ppermute(from_right, axis, left)
+            out = lax.dynamic_update_slice_in_dim(
+                out, from_right, (index + turn) % size * width, axis=dim
+            )
+    return out
+
+
 def body(student, projector, teacher, layer_index, valid_mask):
     rows_dev = student.shape[0]
     feat_dim = student.shape[1]
     chosen = teacher[0]
     chosen = jnp.where((layer_index == 1)[:, None], teacher[1], chosen)
     weight = valid_mask.astype(jnp.float32)[:, None]
-    gathered = lax.all_gather(projector, "seq", axis=1, tiled=True)
+    gathered = gather_around(projector, "seq", 1)
     flat_rows = gathered.reshape(-1, feat_dim)
     predicted = lax.dot_general(
         student, flat_rows, (((1,), (1,)), ((), ())), preferred_element_type=jnp.float32

time: 260 us -> 409 us (1.57)
  starting transfers between devices: 0.08 us -> 96.8 us
  local copies, waits for them, and re-layouts: 0.6 us -> 43.8 us
  waiting for transfers between devices: 205 us -> 228 us
  matrix products: 33 us -> 19.5 us
    ppermute x0 -> x15, waiting for transfers between devices: none -> 221 us  [the longest x8 167 us: gather_around(): from_left = lax.ppermute(from_left, axis, right)]
    all_gather x1 -> x0, waiting for transfers between devices: 201 us -> none  [body(): gathered = lax.all_gather(projector, 'seq', axis=1, tiled=True)]
    ppermute x0 -> x15, starting transfers between devices: none -> 96.8 us  [the longest x7 83.9 us: gather_around(): from_right = lax.ppermute(from_right, axis, left)]
    dynamic_update_slice x0 -> x16, local copies, waits for them, and re-layouts: none -> 26.5 us  [the longest x8 13.9 us: gather_around(): lax.dynamic_update_slice_in_dim(out, from_left, (index - turn) % size * w...]
    dot_general x1, matrix products: 19.6 us -> 9.33 us  [body(): lax.dot_general(student, flat_rows, (((1,), (1,)), ((), ())), preferred_e...]
    unnamed x7 -> x19, local copies, waits for them, and re-layouts: 0.6 us -> 7.17 us
    reshape x0 -> x1, local copies, waits for them, and re-layouts: none -> 6.18 us  [body(): flat_rows = gathered.reshape(-1, feat_dim)]
  transfers between devices with their start and end apart: 2 -> 16, of which waited for: 2 -> 9; matrix products, arithmetic and copies ran while one was open for 1% -> 11% of each run, Pallas kernels for 0% -> 0%
where the time goes in v1:
time: 409 us; the launch traced here: 408 us
  waiting for transfers between devices  228 us (56%)
  starting transfers between devices  96.8 us (24%)
  local copies, waits for them, and re-layouts  43.8 us (11%)
  matrix products  19.5 us (5%)
  between operations  14.8 us (4%)
    ppermute x8, waiting for transfers between devices, gather_around(): from_left = lax.ppermute(from_left, axis, right)  167 us
    ppermute x7, starting transfers between devices, gather_around(): from_right = lax.ppermute(from_right, axis, left)  83.9 us
    ppermute x7, waiting for transfers between devices, gather_around(): from_right = lax.ppermute(from_right, axis, left)  54.1 us
    dynamic_update_slice x8, local copies, waits for them, and re-layouts, gather_around(): lax.dynamic_update_slice_in_dim(out, from_left, (index - turn) % size * w...  13.9 us
    ppermute x8, starting transfers between devices, gather_around(): from_left = lax.ppermute(from_left, axis, right)  12.9 us
    dynamic_update_slice x7, local copies, waits for them, and re-layouts, gather_around(): lax.dynamic_update_slice_in_dim(out, from_right, (index + turn) % size *...  11.6 us
    dot_general x1, matrix products, body(): jnp.dot(masked_err, flat_rows, preferred_element_type=jnp.float32)  10.2 us
    dot_general x1, matrix products, body(): lax.dot_general(student, flat_rows, (((1,), (1,)), ((), ())), preferred_e...  9.33 us
  transfers between devices with their start and end apart: 16, of which 9 were waited for; matrix products, arithmetic and copies ran while one was open for 11% of the time, Pallas kernels for 0%

profile of v1, /device:TPU:0, one launch (start us, length us, event | category | flops | bytes accessed | tf_op | source)
XLA Modules:
  0.0 408.3 jit_solution(14181497634271834836)
XLA Ops:
  7.2 3.0 collective-permute-start
  10.2 4.1 collective-permute-start.1
  14.3 42.5 %collective-permute-done = bf16[1,264,2048]{2,1,0:T(8,128)(2,1)S(1)} collective-permute-done((bf16[1,264,2048]{2,1,0:T(8,128)(2,1)}, bf16[1,264,2048]{2,1,0:T(8,128)(2,1)S(1)}, u32[]{:S(2)}, u32[]{:S(2)}) %collective-permute-start) | collective-permute-done | bytes 1081376 | tf_op jit(solution)/shard_map/ppermute | solution.py:18
  56.8 2.4 collective-permute-start.2
  59.2 3.2 collective-permute-start.3
  62.5 42.3 %collective-permute-done.2 = bf16[1,264,2048]{2,1,0:T(8,128)(2,1)} collective-permute-done((bf16[1,264,2048]{2,1,0:T(8,128)(2,1)S(1)}, bf16[1,264,2048]{2,1,0:T(8,128)(2,1)}, u32[]{:S(2)}, u32[]{:S(2)}) %collective-permute-start.2) | collective-permute-done | bytes 1081376 | tf_op jit(solution)/shard_map/ppermute | solution.py:18
  104.7 2.6 collective-permute-start.4
  107.3 3.9 fusion.4
  111.3 3.1 collective-permute-start.5
  114.3 6.2 %reshape.73 = bf16[4224,2048]{1,0:T(8,128)(2,1)} broadcast(bf16[]{:T(256)} %constant.114.clone.1), dimensions={} | broadcast | bytes 17301506 | tf_op jit(solution)/shard_map/reshape | solution.py:37
  121.6 30.6 %collective-permute-done.4 = bf16[1,264,2048]{2,1,0:T(8,128)(2,1)} collective-permute-done((bf16[1,264,2048]{2,1,0:T(8,128)(2,1)}, bf16[1,264,2048]{2,1,0:T(8,128)(2,1)}, u32[]{:S(2)}, u32[]{:S(2)}) %collective-permute-start.4) | collective-permute-done | bytes 1081376 | tf_op jit(solution)/shard_map/ppermute | solution.py:18
  152.2 2.5 collective-permute-start.6
  154.7 4.1 %copy.11 = bf16[1,256,4224]{1,2,0:T(8,128)(2,1)} copy(bf16[1,256,4224]{2,1,0:T(8,128)(2,1)} %get-tuple-element.2) | data formatting | bytes 4325376
  158.9 2.4 copy.12
  161.3 2.3 bitcast_dynamic-update-slice_fusion.14
  163.6 3.2 collective-permute-start.7
  169.1 30.3 %collective-permute-done.6 = bf16[1,264,2048]{2,1,0:T(8,128)(2,1)} collective-permute-done((bf16[1,264,2048]{2,1,0:T(8,128)(2,1)}, bf16[1,264,2048]{2,1,0:T(8,128)(2,1)}, u32[]{:S(2)}, u32[]{:S(2)}) %collective-permute-start.6) | collective-permute-done | bytes 1081376 | tf_op jit(solution)/shard_map/ppermute | solution.py:18
  199.4 2.5 collective-permute-start.8
  201.9 2.4 bitcast_dynamic-update-slice_fusion.12
  204.3 2.4 bitcast_dynamic-update-slice_fusion.11
  206.7 19.6 %collective-permute-start.9 = (bf16[1,264,2048]{2,1,0:T(8,128)(2,1)S(1)}, bf16[1,264,2048]{2,1,0:T(8,128)(2,1)S(1)}, u32[]{:S(2)}, u32[]{:S(2)}) collective-permute-start(bf16[1,264,2048]{2,1,0:T(8,128)(2,1)S(1)} %collective-permute-done.7), channel_id=1, source_target_pairs={{0,30},{2,0},{4,2},{6,4},{8,6},{10,8},{12,10},{14,12},{16,14},{18,... | collective-permute-start | bytes 3244040 | tf_op jit(solution)/shard_map/ppermute | solution.py:23
  230.9 2.3 bitcast_dynamic-update-slice_fusion.8
  233.3 16.8 %collective-permute-done.9 = bf16[1,264,2048]{2,1,0:T(8,128)(2,1)S(1)} collective-permute-done((bf16[1,264,2048]{2,1,0:T(8,128)(2,1)S(1)}, bf16[1,264,2048]{2,1,0:T(8,128)(2,1)S(1)}, u32[]{:S(2)}, u32[]{:S(2)}) %collective-permute-start.9) | collective-permute-done | bytes 1081376 | tf_op jit(solution)/shard_map/ppermute | solution.py:23
  250.1 25.0 %collective-permute-start.11 = (bf16[1,264,2048]{2,1,0:T(8,128)(2,1)S(1)}, bf16[1,264,2048]{2,1,0:T(8,128)(2,1)S(1)}, u32[]{:S(2)}, u32[]{:S(2)}) collective-permute-start(bf16[1,264,2048]{2,1,0:T(8,128)(2,1)S(1)} %collective-permute-done.9), channel_id=1, source_target_pairs={{0,30},{2,0},{4,2},{6,4},{8,6},{10,8},{12,10},{14,12},{16,14},{18,... | collective-permute-start | bytes 3244040 | tf_op jit(solution)/shard_map/ppermute | solution.py:23
  278.5 19.1 %collective-permute-done.11 = bf16[1,264,2048]{2,1,0:T(8,128)(2,1)S(1)} collective-permute-done((bf16[1,264,2048]{2,1,0:T(8,128)(2,1)S(1)}, bf16[1,264,2048]{2,1,0:T(8,128)(2,1)S(1)}, u32[]{:S(2)}, u32[]{:S(2)}) %collective-permute-start.11) | collective-permute-done | bytes 1081376 | tf_op jit(solution)/shard_map/ppermute | solution.py:23
  297.6 25.7 %collective-permute-start.13 = (bf16[1,264,2048]{2,1,0:T(8,128)(2,1)S(1)}, bf16[1,264,2048]{2,1,0:T(8,128)(2,1)S(1)}, u32[]{:S(2)}, u32[]{:S(2)}) collective-permute-start(bf16[1,264,2048]{2,1,0:T(8,128)(2,1)S(1)} %collective-permute-done.11), channel_id=1, source_target_pairs={{0,30},{2,0},{4,2},{6,4},{8,6},{10,8},{12,10},{14,12},{16,14},{18,... | collective-permute-start | bytes 3244040 | tf_op jit(solution)/shard_map/ppermute | solution.py:23
  326.6 18.2 %collective-permute-done.13 = bf16[1,264,2048]{2,1,0:T(8,128)(2,1)S(1)} collective-permute-done((bf16[1,264,2048]{2,1,0:T(8,128)(2,1)S(1)}, bf16[1,264,2048]{2,1,0:T(8,128)(2,1)S(1)}, u32[]{:S(2)}, u32[]{:S(2)}) %collective-permute-start.13) | collective-permute-done | bytes 1081376 | tf_op jit(solution)/shard_map/ppermute | solution.py:23
  346.0 21.6 %collective-permute-done.14 = bf16[1,264,2048]{2,1,0:T(8,128)(2,1)S(1)} collective-permute-done((bf16[1,264,2048]{2,1,0:T(8,128)(2,1)S(1)}, bf16[1,264,2048]{2,1,0:T(8,128)(2,1)S(1)}, u32[]{:S(2)}, u32[]{:S(2)}) %collective-permute-start.14) | collective-permute-done | bytes 1081376 | tf_op jit(solution)/shard_map/ppermute | solution.py:18
  368.8 9.3 %multiply_reduce_fusion = (f32[256]{0:T(256)S(1)}, f32[256,4224]{0,1:T(8,128)S(1)}) fusion(bf16[1,256,4224]{1,2,0:T(8,128)(2,1)S(1)} %copy-done.2, bf16[1,256,4224]{1,2,0:T(8,128)(2,1)S(1)} %copy-done.1, pred[256]{0:T(512)(128)(4,1)S(1)} %broadcast_compare_fusion, bf16[4224,2048]{1,0:T(8,128)(2,1)} %bitcast_dynamic-update-slice_fusion, ...), kind=kOutput, calls=%fused_computation.2 | convolution fusion | flops 4434591744 | bytes 27002112 | tf_op jit(solution)/shard_map/dot_general | solution.py:38
  378.1 10.2 %fusion.1 = f32[256,2048]{1,0:T(8,128)} fusion(bf16[4224,2048]{1,0:T(8,128)(2,1)} %bitcast_dynamic-update-slice_fusion, f32[256,4224]{0,1:T(8,128)S(1)} %get-tuple-element.5, f32[256]{0:T(256)S(1)} %convert_element_type.15), kind=kOutput, calls=%fused_computation.4 | convolution fusion | flops 4431347712 | bytes 23725056 | tf_op jit(solution)/shard_map/dot_general | solution.py:43
  389.6 2.5 all-reduce
  392.7 6.7 %reduce-scatter.2.cloned.1.call-done = f32[256,1024]{1,0:T(8,128)} async-done(((f32[256,2048]{1,0:T(8,128)}), f32[256,1024]{1,0:T(8,128)}) %reduce-scatter.2.cloned.1.call-update) | async-done | bytes 1048592 | tf_op jit(solution)/shard_map/reduce_scatter | solution.py:46
  (45 shorter events, 20.5 us)
Async XLA Ops:
  7.2 361.6 %copy-start = (bf16[256,2048]{1,0:T(8,128)(2,1)S(1)}, bf16[256,2048]{1,0:T(8,128)(2,1)}, u32[]{:S(2)}) copy-start(bf16[256,2048]{1,0:T(8,128)(2,1)} %param.5) | copy-start | bytes 3145732
  7.2 392.2 %reduce-scatter.2.cloned.1.call-start = ((), (), s32[]{:S(2)}) async-start(), calls=%async_computation.1 | async-start | bytes 3145728 | tf_op jit(solution)/shard_map/reduce_scatter | solution.py:46
  7.2 49.6 %collective-permute-start = (bf16[1,264,2048]{2,1,0:T(8,128)(2,1)}, bf16[1,264,2048]{2,1,0:T(8,128)(2,1)S(1)}, u32[]{:S(2)}, u32[]{:S(2)}) collective-permute-start(bf16[1,264,2048]{2,1,0:T(8,128)(2,1)} %param.6), channel_id=1, source_target_pairs={{0,2},{2,4},{4,6},{6,8},{8,10},{10,12},{12,14},{14,16},{16,18},{18... | collective-permute-start | bytes 3244040 | tf_op jit(solution)/shard_map/ppermute | solution.py:18
  10.2 49.0 %collective-permute-start.1 = (bf16[1,264,2048]{2,1,0:T(8,128)(2,1)}, bf16[1,264,2048]{2,1,0:T(8,128)(2,1)}, u32[]{:S(2)}, u32[]{:S(2)}) collective-permute-start(bf16[1,264,2048]{2,1,0:T(8,128)(2,1)} %param.6), channel_id=1, source_target_pairs={{0,30},{2,0},{4,2},{6,4},{8,6},{10,8},{12,10},{14,12},{16,14},{18,... | collective-permute-start | bytes 3244040 | tf_op jit(solution)/shard_map/ppermute | solution.py:23
  56.8 47.9 %copy-start.4 = (bf16[1,264,2048]{2,1,0:T(8,128)(2,1)}, bf16[1,264,2048]{2,1,0:T(8,128)(2,1)S(1)}, u32[]{:S(2)}) copy-start(bf16[1,264,2048]{2,1,0:T(8,128)(2,1)S(1)} %collective-permute-done) | copy-start | bytes 3244036
  56.8 47.9 %collective-permute-start.2 = (bf16[1,264,2048]{2,1,0:T(8,128)(2,1)S(1)}, bf16[1,264,2048]{2,1,0:T(8,128)(2,1)}, u32[]{:S(2)}, u32[]{:S(2)}) collective-permute-start(bf16[1,264,2048]{2,1,0:T(8,128)(2,1)S(1)} %collective-permute-done), channel_id=1, source_target_pairs={{0,2},{2,4},{4,6},{6,8},{8,10},{10,12},{12,14},{14,16},{16,18},{18... | collective-permute-start | bytes 3244040 | tf_op jit(solution)/shard_map/ppermute | solution.py:18
  59.2 52.0 %collective-permute-start.3 = (bf16[1,264,2048]{2,1,0:T(8,128)(2,1)}, bf16[1,264,2048]{2,1,0:T(8,128)(2,1)}, u32[]{:S(2)}, u32[]{:S(2)}) collective-permute-start(bf16[1,264,2048]{2,1,0:T(8,128)(2,1)} %collective-permute-done.1), channel_id=1, source_target_pairs={{0,30},{2,0},{4,2},{6,4},{8,6},{10,8},{12,10},{14,12},{16,14},{18,... | collective-permute-start | bytes 3244040 | tf_op jit(solution)/shard_map/ppermute | solution.py:23
  104.7 47.5 %collective-permute-start.4 = (bf16[1,264,2048]{2,1,0:T(8,128)(2,1)}, bf16[1,264,2048]{2,1,0:T(8,128)(2,1)}, u32[]{:S(2)}, u32[]{:S(2)}) collective-permute-start(bf16[1,264,2048]{2,1,0:T(8,128)(2,1)} %collective-permute-done.2), channel_id=1, source_target_pairs={{0,2},{2,4},{4,6},{6,8},{8,10},{10,12},{12,14},{14,16},{16,18},{18... | collective-permute-start | bytes 3244040 | tf_op jit(solution)/shard_map/ppermute | solution.py:18
  111.2 9.3 %copy-start.3 = (bf16[1,264,2048]{2,1,0:T(8,128)(2,1)S(1)}, bf16[1,264,2048]{2,1,0:T(8,128)(2,1)}, u32[]{:S(2)}) copy-start(bf16[1,264,2048]{2,1,0:T(8,128)(2,1)} %param.6) | copy-start | bytes 3244036
  111.2 43.5 %copy-start.6 = (s32[256]{0:T(256)S(1)}, s32[256]{0:T(256)}, u32[]{:S(2)}) copy-start(s32[256]{0:T(256)} %param.8) | copy-start | bytes 3076
  111.3 52.4 %collective-permute-start.5 = (bf16[1,264,2048]{2,1,0:T(8,128)(2,1)}, bf16[1,264,2048]{2,1,0:T(8,128)(2,1)}, u32[]{:S(2)}, u32[]{:S(2)}) collective-permute-start(bf16[1,264,2048]{2,1,0:T(8,128)(2,1)} %collective-permute-done.3), channel_id=1, source_target_pairs={{0,30},{2,0},{4,2},{6,4},{8,6},{10,8},{12,10},{14,12},{16,14},{18,... | collective-permute-start | bytes 3244040 | tf_op jit(solution)/shard_map/ppermute | solution.py:23
  152.2 47.2 %collective-permute-start.6 = (bf16[1,264,2048]{2,1,0:T(8,128)(2,1)}, bf16[1,264,2048]{2,1,0:T(8,128)(2,1)}, u32[]{:S(2)}, u32[]{:S(2)}) collective-permute-start(bf16[1,264,2048]{2,1,0:T(8,128)(2,1)} %collective-permute-done.4), channel_id=1, source_target_pairs={{0,2},{2,4},{4,6},{6,8},{8,10},{10,12},{12,14},{14,16},{16,18},{18... | collective-permute-start | bytes 3244040 | tf_op jit(solution)/shard_map/ppermute | solution.py:18
  154.7 6.6 %copy-start.5 = (s32[256]{0:T(256)S(1)}, s32[256]{0:T(256)}, u32[]{:S(2)}) copy-start(s32[256]{0:T(256)} %param.9) | copy-start | bytes 3076
  163.6 43.0 %collective-permute-start.7 = (bf16[1,264,2048]{2,1,0:T(8,128)(2,1)}, bf16[1,264,2048]{2,1,0:T(8,128)(2,1)S(1)}, u32[]{:S(2)}, u32[]{:S(2)}) collective-permute-start(bf16[1,264,2048]{2,1,0:T(8,128)(2,1)} %collective-permute-done.5), channel_id=1, source_target_pairs={{0,30},{2,0},{4,2},{6,4},{8,6},{10,8},{12,10},{14,12},{16,14},{18,... | collective-permute-start | bytes 3244040 | tf_op jit(solution)/shard_map/ppermute | solution.py:23
  199.4 29.2 %collective-permute-start.8 = (bf16[1,264,2048]{2,1,0:T(8,128)(2,1)}, bf16[1,264,2048]{2,1,0:T(8,128)(2,1)S(1)}, u32[]{:S(2)}, u32[]{:S(2)}) collective-permute-start(bf16[1,264,2048]{2,1,0:T(8,128)(2,1)} %collective-permute-done.6), channel_id=1, source_target_pairs={{0,2},{2,4},{4,6},{6,8},{8,10},{10,12},{12,14},{14,16},{16,18},{18... | collective-permute-start | bytes 3244040 | tf_op jit(solution)/shard_map/ppermute | solution.py:18
  206.7 43.4 %collective-permute-start.9 = (bf16[1,264,2048]{2,1,0:T(8,128)(2,1)S(1)}, bf16[1,264,2048]{2,1,0:T(8,128)(2,1)S(1)}, u32[]{:S(2)}, u32[]{:S(2)}) collective-permute-start(bf16[1,264,2048]{2,1,0:T(8,128)(2,1)S(1)} %collective-permute-done.7), channel_id=1, source_target_pairs={{0,30},{2,0},{4,2},{6,4},{8,6},{10,8},{12,10},{14,12},{16,14},{18,... | collective-permute-start | bytes 3244040 | tf_op jit(solution)/shard_map/ppermute | solution.py:23
  228.6 47.7 %collective-permute-start.10 = (bf16[1,264,2048]{2,1,0:T(8,128)(2,1)S(1)}, bf16[1,264,2048]{2,1,0:T(8,128)(2,1)S(1)}, u32[]{:S(2)}, u32[]{:S(2)}) collective-permute-start(bf16[1,264,2048]{2,1,0:T(8,128)(2,1)S(1)} %collective-permute-done.8), channel_id=1, source_target_pairs={{0,2},{2,4},{4,6},{6,8},{8,10},{10,12},{12,14},{14,16},{16,18},{18... | collective-permute-start | bytes 3244040 | tf_op jit(solution)/shard_map/ppermute | solution.py:18
  250.1 47.5 %collective-permute-start.11 = (bf16[1,264,2048]{2,1,0:T(8,128)(2,1)S(1)}, bf16[1,264,2048]{2,1,0:T(8,128)(2,1)S(1)}, u32[]{:S(2)}, u32[]{:S(2)}) collective-permute-start(bf16[1,264,2048]{2,1,0:T(8,128)(2,1)S(1)} %collective-permute-done.9), channel_id=1, source_target_pairs={{0,30},{2,0},{4,2},{6,4},{8,6},{10,8},{12,10},{14,12},{16,14},{18,... | collective-permute-start | bytes 3244040 | tf_op jit(solution)/shard_map/ppermute | solution.py:23
  276.3 48.1 %collective-permute-start.12 = (bf16[1,264,2048]{2,1,0:T(8,128)(2,1)S(1)}, bf16[1,264,2048]{2,1,0:T(8,128)(2,1)S(1)}, u32[]{:S(2)}, u32[]{:S(2)}) collective-permute-start(bf16[1,264,2048]{2,1,0:T(8,128)(2,1)S(1)} %collective-permute-done.10), channel_id=1, source_target_pairs={{0,2},{2,4},{4,6},{6,8},{8,10},{10,12},{12,14},{14,16},{16,18},{18... | collective-permute-start | bytes 3244040 | tf_op jit(solution)/shard_map/ppermute | solution.py:18
  297.6 47.2 %collective-permute-start.13 = (bf16[1,264,2048]{2,1,0:T(8,128)(2,1)S(1)}, bf16[1,264,2048]{2,1,0:T(8,128)(2,1)S(1)}, u32[]{:S(2)}, u32[]{:S(2)}) collective-permute-start(bf16[1,264,2048]{2,1,0:T(8,128)(2,1)S(1)} %collective-permute-done.11), channel_id=1, source_target_pairs={{0,30},{2,0},{4,2},{6,4},{8,6},{10,8},{12,10},{14,12},{16,14},{18,... | collective-permute-start | bytes 3244040 | tf_op jit(solution)/shard_map/ppermute | solution.py:23
  324.3 44.4 %copy-start.1 = (bf16[1,256,4224]{1,2,0:T(8,128)(2,1)S(1)}, bf16[1,256,4224]{1,2,0:T(8,128)(2,1)}, u32[]{:S(2)}) copy-start(bf16[1,256,4224]{1,2,0:T(8,128)(2,1)} %copy.11) | copy-start | bytes 6488068
  324.3 44.4 %copy-start.2 = (bf16[1,256,4224]{1,2,0:T(8,128)(2,1)S(1)}, bf16[1,256,4224]{1,2,0:T(8,128)(2,1)}, u32[]{:S(2)}) copy-start(bf16[1,256,4224]{1,2,0:T(8,128)(2,1)} %copy.12) | copy-start | bytes 6488068
  324.3 43.3 %collective-permute-start.14 = (bf16[1,264,2048]{2,1,0:T(8,128)(2,1)S(1)}, bf16[1,264,2048]{2,1,0:T(8,128)(2,1)S(1)}, u32[]{:S(2)}, u32[]{:S(2)}) collective-permute-start(bf16[1,264,2048]{2,1,0:T(8,128)(2,1)S(1)} %collective-permute-done.12), channel_id=1, source_target_pairs={{0,2},{2,4},{4,6},{6,8},{8,10},{10,12},{12,14},{14,16},{16,18},{18... | collective-permute-start | bytes 3244040 | tf_op jit(solution)/shard_map/ppermute | solution.py:18
  378.1 10.3 %copy-start.7 = (u32[32]{0:T(128)S(1)}, u32[32]{0:T(128)}, u32[]{:S(2)}) copy-start(u32[32]{0:T(128)} %constant.144) | copy-start | bytes 388
Sparse Core Ops, SparseCore 0:
  388.5 10.8 reduce-scatter.1
